TPU v7x, 256 devices: a whole 4x4x8 slice. The times are simulated.
256 devices in a mesh: section: 4 (over x), dp: 16 (over y, z_lo, core), tensor: 4 (over z_hi).
Axes of the slice: x: 4, y: 4, z: 8 (z_hi: 4, z_lo: 2; z = z_hi * 2 + z_lo), core: 2. Of those that a mesh axis runs over, the one named last changes fastest.
Arguments:
- inputs: bfloat16 [4, 1024, 1024], P(None, ('dp', 'tensor')), may hold values from -16 to 16
- gains: float32 [4, 1024], P('section'), may hold values from 0.1 to 1.9
- w_up: bfloat16 [4, 1024, 4096], P('section', None, 'tensor'), may hold values from -0.1875 to 0.1875
- w_down: bfloat16 [4, 4096, 1024], P('section', 'tensor'), may hold values from -0.09375 to 0.09375
- out_grad: bfloat16 [4, 1024, 1024], P(None, ('dp', 'tensor')), may hold values from -0.5 to 0.5
Outputs:
- up_grads: float32 [4, 1024, 4096], P('section', 'dp', 'tensor')
- down_grads: float32 [4, 4096, 1024], P('section', 'tensor', 'dp')
- gain_grads: float32 [4, 1024], P('section', ('dp', 'tensor'))
All inputs are finite; a program needn't handle non-finite values.
Results may differ from a plain program's by a relative error of at most 0.035.
Values may be sent and summed in bfloat16 or wider, within the bound.
A program may use at most 64 MiB of HBM per device.

v0:
```python
import math

import jax
import jax.numpy as jnp
from jax import lax
from jax.sharding import PartitionSpec as P

norm_eps = 1e-05
gelu_coef = 0.044715


def shifted(value, axis, steps):
    count = lax.axis_size(axis)
    initial, last = (max(0, -steps), min(count, count - steps))
    return lax.ppermute(value, axis, [(source, source + steps) for source in range(initial, last)])


def normalize(hidden):
    values = hidden.astype(jnp.float32)
    centre = values - jnp.mean(values, axis=-1, keepdims=True)
    spread = jnp.mean(centre * centre, axis=-1, keepdims=True)
    scale = lax.rsqrt(spread + norm_eps)
    return (centre * scale, scale)


def gelu_slope(preact):
    root = math.sqrt(2.0 / math.pi)
    inner = root * (preact + gelu_coef * preact * preact * preact)
    tangent = jnp.tanh(inner)
    return 0.5 * (1.0 + tangent) + 0.5 * preact * (1.0 - tangent * tangent) * root * (
        1.0 + 3.0 * gelu_coef * preact * preact
    )


def norm_back(upstream, normed, scale, gain_row):
    scaled = upstream * gain_row
    return scale * (
        scaled
        - jnp.mean(scaled, axis=-1, keepdims=True)
        - normed * jnp.mean(scaled * normed, axis=-1, keepdims=True)
    )


def contract_rows(left, right):
    return lax.dot_general(
        left, right, (((0,), (0,)), ((), ())), preferred_element_type=jnp.float32
    )


def contract_cols(left, right):
    return lax.dot_general(
        left, right, (((1,), (1,)), ((), ())), preferred_element_type=jnp.float32
    )


def pick(stack, slot):
    return lax.dynamic_index_in_dim(stack, slot, 0, keepdims=False)


def store(stack, value, slot, valid):
    kept = jnp.where(valid, value, pick(stack, slot))
    return lax.dynamic_update_index_in_dim(stack, kept, slot, 0)


def regather(rows_in, gain_row, up_local):
    normed, scale = normalize(rows_in)
    norm_rows = (normed * gain_row).astype(jnp.bfloat16)
    norm_full = lax.all_gather(norm_rows, "tensor", axis=0, tiled=True)
    return (norm_full, jnp.dot(norm_full, up_local, preferred_element_type=jnp.float32))


def per_device(inputs, gains, w_up, w_down, out_grad):
    section_count = lax.axis_size("section")
    section_pos = lax.axis_index("section")
    micro, rows, width = inputs.shape
    gain_row = gains[0]
    up_local = w_up[0]
    down_local = w_down[0]
    full_rows = rows * lax.axis_size("tensor")
    hidden_local = up_local.shape[1]
    ticks = micro + section_count - 1
    own_stash = jnp.zeros((micro, rows, width), jnp.bfloat16)
    norm_stash = jnp.zeros((micro, full_rows, width), jnp.bfloat16)
    outgoing = jnp.zeros((rows, width), jnp.bfloat16)
    for tick in range(ticks):
        arrived = shifted(outgoing, "section", 1)
        slot = tick - section_pos
        valid = (slot >= 0) & (slot < micro)
        slot = jnp.clip(slot, 0, micro - 1)
        rows_in = jnp.where(section_pos == 0, inputs[min(tick, micro - 1)], arrived)
        normed, scale = normalize(rows_in)
        norm_rows = (normed * gain_row).astype(jnp.bfloat16)
        norm_full = lax.all_gather(norm_rows, "tensor", axis=0, tiled=True)
        preact = jnp.dot(norm_full, up_local, preferred_element_type=jnp.float32)
        activated = jax.nn.gelu(preact, approximate=True).astype(jnp.bfloat16)

        def down_term(start, count, activated=activated):
            return jnp.dot(activated, down_local, preferred_element_type=jnp.float32)

        mixed = lax.psum_scatter(
            down_term(jnp.int32(0), rows * lax.axis_size("tensor")).astype(jnp.bfloat16),
            "tensor",
            scatter_dimension=0,
            tiled=True,
        ).astype(jnp.float32)
        outgoing = (rows_in.astype(jnp.float32) + mixed).astype(jnp.bfloat16)
        own_stash = store(own_stash, rows_in, slot, valid)
    returning = jnp.zeros((rows, width), jnp.bfloat16)
    grad_stash = jnp.zeros((micro, full_rows, width), jnp.bfloat16)
    activated_stash = jnp.zeros((micro, full_rows, hidden_local), jnp.bfloat16)
    preact_grad_stash = jnp.zeros((micro, full_rows, hidden_local), jnp.bfloat16)
    gain_total = jnp.zeros((width,), jnp.float32)
    for tick in range(ticks):
        arrived = shifted(returning, "section", -1)
        slot = tick - (section_count - 1 - section_pos)
        valid = (slot >= 0) & (slot < micro)
        slot = jnp.clip(slot, 0, micro - 1)
        grad_rows = jnp.where(
            section_pos == section_count - 1, out_grad[min(tick, micro - 1)], arrived
        )
        rows_in = pick(own_stash, slot)
        norm_full, preact = regather(rows_in, gain_row, up_local)
        norm_stash = store(norm_stash, norm_full, slot, valid)
        normed, scale = normalize(rows_in)
        grad_full = lax.all_gather(grad_rows, "tensor", axis=0, tiled=True)
        down_grad = contract_cols(grad_full, down_local)
        preact_grad = (down_grad * gelu_slope(preact)).astype(jnp.bfloat16)

        def up_term(start, count, preact_grad=preact_grad):
            return contract_cols(preact_grad, up_local)

        norm_grad = lax.psum_scatter(
            up_term(jnp.int32(0), rows * lax.axis_size("tensor")).astype(jnp.bfloat16),
            "tensor",
            scatter_dimension=0,
            tiled=True,
        ).astype(jnp.float32)
        gain_total = gain_total + jnp.where(valid, jnp.sum(norm_grad * normed, axis=0), 0.0)
        returning = (
            grad_rows.astype(jnp.float32) + norm_back(norm_grad, normed, scale, gain_row)
        ).astype(jnp.bfloat16)
        grad_stash = store(grad_stash, grad_full, slot, valid)
        activated_stash = store(
            activated_stash, jax.nn.gelu(preact, approximate=True).astype(jnp.bfloat16), slot, valid
        )
        preact_grad_stash = store(preact_grad_stash, preact_grad, slot, valid)
    up_grad = contract_rows(
        norm_stash.reshape(-1, width), preact_grad_stash.reshape(-1, hidden_local)
    )
    down_grad_w = contract_rows(
        activated_stash.reshape(-1, hidden_local), grad_stash.reshape(-1, width)
    )
    up_share, down_share = (
        lax.psum_scatter(
            up_grad[None].astype(jnp.bfloat16), "dp", scatter_dimension=1, tiled=True
        ).astype(jnp.float32),
        lax.psum_scatter(
            down_grad_w[None].astype(jnp.bfloat16), "dp", scatter_dimension=2, tiled=True
        ).astype(jnp.float32),
    )
    gain_share = lax.psum_scatter(
        gain_total[None], ("dp", "tensor"), scatter_dimension=1, tiled=True
    )
    return (up_share, down_share, gain_share)


def solution(mesh):
    placed = (
        P(None, ("dp", "tensor"), None),
        P("section", None),
        P("section", None, "tensor"),
        P("section", "tensor", None),
        P(None, ("dp", "tensor"), None),
    )
    return jax.shard_map(
        per_device,
        mesh=mesh,
        in_specs=placed,
        out_specs=(
            P("section", "dp", "tensor"),
            P("section", "tensor", "dp"),
            P("section", ("dp", "tensor")),
        ),
        check_vma=False,
    )
```

profile of v0, /device:TPU:1, one launch (start us, length us, event | category | flops | bytes accessed | tf_op | source)
XLA Modules:
  0.0 1112.0 jit_solution(4539508983205165038)
XLA Ops:
  14.2 14.9 %all_gather.60 = bf16[64,1024]{1,0:T(8,128)(2,1)S(1)} all-gather(bf16[16,1024]{1,0:T(8,128)(2,1)S(1)} %fusion.401), channel_id=1, replica_groups=mesh['section'=4,'dp'=16,'tensor'=4] {'tensor'}, dimensions={0}, use_global_device_ids=true | all-gather | bytes 163840 | tf_op jit(solution)/shard_map/all_gather | solution.py:93
  32.4 26.7 %reduce-scatter.21.cloned.1.call-done = bf16[16,1024]{1,0:T(8,128)(2,1)} async-done(((bf16[64,1024]{1,0:T(8,128)(2,1)}), bf16[16,1024]{1,0:T(8,128)(2,1)}) %reduce-scatter.21.cloned.1.call-update) | async-done | bytes 32784 | tf_op jit(solution)/shard_map/reduce_scatter | solution.py:100
  90.7 16.2 %reduce-scatter.23.cloned.1.call-done = bf16[16,1024]{1,0:T(8,128)(2,1)} async-done(((bf16[64,1024]{1,0:T(8,128)(2,1)}), bf16[16,1024]{1,0:T(8,128)(2,1)}) %reduce-scatter.23.cloned.1.call-update) | async-done | bytes 32784 | tf_op jit(solution)/shard_map/reduce_scatter | solution.py:100
  112.3 11.0 all_gather.62
  127.2 27.1 %reduce-scatter.25.cloned.1.call-done = bf16[16,1024]{1,0:T(8,128)(2,1)} async-done(((bf16[64,1024]{1,0:T(8,128)(2,1)}), bf16[16,1024]{1,0:T(8,128)(2,1)}) %reduce-scatter.25.cloned.1.call-update) | async-done | bytes 32784 | tf_op jit(solution)/shard_map/reduce_scatter | solution.py:100
  159.6 10.9 all_gather.63
  173.8 28.0 %reduce-scatter.27.cloned.1.call-done = bf16[16,1024]{1,0:T(8,128)(2,1)} async-done(((bf16[64,1024]{1,0:T(8,128)(2,1)}), bf16[16,1024]{1,0:T(8,128)(2,1)}) %reduce-scatter.27.cloned.1.call-update) | async-done | bytes 32784 | tf_op jit(solution)/shard_map/reduce_scatter | solution.py:100
  207.1 11.0 all_gather.64
  221.3 27.9 %reduce-scatter.29.cloned.1.call-done = bf16[16,1024]{1,0:T(8,128)(2,1)} async-done(((bf16[64,1024]{1,0:T(8,128)(2,1)}), bf16[16,1024]{1,0:T(8,128)(2,1)}) %reduce-scatter.29.cloned.1.call-update) | async-done | bytes 32784 | tf_op jit(solution)/shard_map/reduce_scatter | solution.py:100
  268.7 28.0 %reduce-scatter.31.cloned.1.call-done = bf16[16,1024]{1,0:T(8,128)(2,1)} async-done(((bf16[64,1024]{1,0:T(8,128)(2,1)}), bf16[16,1024]{1,0:T(8,128)(2,1)}) %reduce-scatter.31.cloned.1.call-update) | async-done | bytes 32784 | tf_op jit(solution)/shard_map/reduce_scatter | solution.py:100
  302.7 11.2 %all_gather.66 = bf16[64,1024]{1,0:T(8,128)(2,1)S(1)} all-gather(bf16[16,1024]{1,0:T(8,128)(2,1)S(1)} %fusion.407), channel_id=1, replica_groups=mesh['section'=4,'dp'=16,'tensor'=4] {'tensor'}, dimensions={0}, use_global_device_ids=true | all-gather | bytes 163840 | tf_op jit(solution)/shard_map/all_gather | solution.py:68
  317.7 27.2 %reduce-scatter.33.cloned.1.call-done = bf16[16,1024]{1,0:T(8,128)(2,1)} async-done(((bf16[64,1024]{1,0:T(8,128)(2,1)}), bf16[16,1024]{1,0:T(8,128)(2,1)}) %reduce-scatter.33.cloned.1.call-update) | async-done | bytes 32784 | tf_op jit(solution)/shard_map/reduce_scatter | solution.py:132
  381.1 26.8 %reduce-scatter.35.cloned.1.call-done = bf16[16,1024]{1,0:T(8,128)(2,1)} async-done(((bf16[64,1024]{1,0:T(8,128)(2,1)}), bf16[16,1024]{1,0:T(8,128)(2,1)}) %reduce-scatter.35.cloned.1.call-update) | async-done | bytes 32784 | tf_op jit(solution)/shard_map/reduce_scatter | solution.py:132
  411.3 11.1 all_gather.68
  425.3 11.0 all_gather.75
  442.4 26.7 %reduce-scatter.37.cloned.1.call-done = bf16[16,1024]{1,0:T(8,128)(2,1)} async-done(((bf16[64,1024]{1,0:T(8,128)(2,1)}), bf16[16,1024]{1,0:T(8,128)(2,1)}) %reduce-scatter.37.cloned.1.call-update) | async-done | bytes 32784 | tf_op jit(solution)/shard_map/reduce_scatter | solution.py:132
  503.4 26.7 %reduce-scatter.39.cloned.1.call-done = bf16[16,1024]{1,0:T(8,128)(2,1)} async-done(((bf16[64,1024]{1,0:T(8,128)(2,1)}), bf16[16,1024]{1,0:T(8,128)(2,1)}) %reduce-scatter.39.cloned.1.call-update) | async-done | bytes 32784 | tf_op jit(solution)/shard_map/reduce_scatter | solution.py:132
  564.9 26.7 %reduce-scatter.41.cloned.1.call-done = bf16[16,1024]{1,0:T(8,128)(2,1)} async-done(((bf16[64,1024]{1,0:T(8,128)(2,1)}), bf16[16,1024]{1,0:T(8,128)(2,1)}) %reduce-scatter.41.cloned.1.call-update) | async-done | bytes 32784 | tf_op jit(solution)/shard_map/reduce_scatter | solution.py:132
  609.2 11.0 all_gather.78
  624.8 28.2 %reduce-scatter.43.cloned.1.call-done = bf16[16,1024]{1,0:T(8,128)(2,1)} async-done(((bf16[64,1024]{1,0:T(8,128)(2,1)}), bf16[16,1024]{1,0:T(8,128)(2,1)}) %reduce-scatter.43.cloned.1.call-update) | async-done | bytes 32784 | tf_op jit(solution)/shard_map/reduce_scatter | solution.py:132
  685.8 27.9 %reduce-scatter.47.cloned.1.call-done = bf16[16,1024]{1,0:T(8,128)(2,1)} async-done(((bf16[64,1024]{1,0:T(8,128)(2,1)}), bf16[16,1024]{1,0:T(8,128)(2,1)}) %reduce-scatter.47.cloned.1.call-update) | async-done | bytes 32784 | tf_op jit(solution)/shard_map/reduce_scatter | solution.py:132
  738.4 235.6 %reduce-scatter.51.cloned.1.call-done = f32[16,1]{1,0:T(8,128)} async-done(((f32[1024,1]{1,0:T(8,128)}), f32[16,1]{1,0:T(8,128)}) %reduce-scatter.51.cloned.1.call-update) | async-done | bytes 80
  975.3 61.0 %reduce-scatter.49.cloned.1.call-done = bf16[64,1024]{1,0:T(8,128)(2,1)} async-done(((bf16[1024,1024]{1,0:T(8,128)(2,1)}), bf16[64,1024]{1,0:T(8,128)(2,1)}) %reduce-scatter.49.cloned.1.call-update) | async-done | bytes 131088
  1038.4 65.5 %reduce-scatter.45.cloned.1.call-done = bf16[1,64,1024]{2,1,0:T(8,128)(2,1)} async-done(((bf16[1,1024,1024]{2,1,0:T(8,128)(2,1)}), bf16[1,64,1024]{2,1,0:T(8,128)(2,1)}) %reduce-scatter.45.cloned.1.call-update) | async-done | bytes 131088 | tf_op jit(solution)/shard_map/reduce_scatter | solution.py:154
  (358 shorter events, 298.6 us)
Async XLA Ops:
  7.2 51.9 %reduce-scatter.21.cloned.1.call-start = ((), (), s32[]{:S(2)}) async-start(), calls=%async_computation.16 | async-start | bytes 163840 | tf_op jit(solution)/shard_map/reduce_scatter | solution.py:100
  7.2 5.1 collective-permute-start
  32.3 74.5 %reduce-scatter.23.cloned.1.call-start = ((), (), s32[]{:S(2)}) async-start(), calls=%async_computation.17 | async-start | bytes 163840 | tf_op jit(solution)/shard_map/reduce_scatter | solution.py:100
  63.0 16.0 %collective-permute-start.7 = (bf16[16,1024]{1,0:T(8,128)(2,1)S(1)}, bf16[16,1024]{1,0:T(8,128)(2,1)S(1)}, u32[]{:S(2)}, u32[]{:S(2)}) collective-permute-start(bf16[16,1024]{1,0:T(8,128)(2,1)S(1)} %broadcast.447), channel_id=1, source_target_pairs={{64,0},{128,64},{192,128},{65,1},{129,65},{193,129},{66,2},{130,66... | collective-permute-start | bytes 98312 | tf_op jit(solution)/shard_map/ppermute | solution.py:15
  78.9 75.4 %reduce-scatter.25.cloned.1.call-start = ((), (), s32[]{:S(2)}) async-start(), calls=%async_computation.18 | async-start | bytes 163840 | tf_op jit(solution)/shard_map/reduce_scatter | solution.py:100
  126.5 75.3 %reduce-scatter.27.cloned.1.call-start = ((), (), s32[]{:S(2)}) async-start(), calls=%async_computation.19 | async-start | bytes 163840 | tf_op jit(solution)/shard_map/reduce_scatter | solution.py:100
  173.7 75.5 %reduce-scatter.29.cloned.1.call-start = ((), (), s32[]{:S(2)}) async-start(), calls=%async_computation.20 | async-start | bytes 163840 | tf_op jit(solution)/shard_map/reduce_scatter | solution.py:100
  221.2 75.5 %reduce-scatter.31.cloned.1.call-start = ((), (), s32[]{:S(2)}) async-start(), calls=%async_computation.21 | async-start | bytes 163840 | tf_op jit(solution)/shard_map/reduce_scatter | solution.py:100
  268.6 76.3 %reduce-scatter.33.cloned.1.call-start = ((), (), s32[]{:S(2)}) async-start(), calls=%async_computation.22 | async-start | bytes 163840 | tf_op jit(solution)/shard_map/reduce_scatter | solution.py:132
  316.9 91.0 %reduce-scatter.35.cloned.1.call-start = ((), (), s32[]{:S(2)}) async-start(), calls=%async_computation.23 | async-start | bytes 163840 | tf_op jit(solution)/shard_map/reduce_scatter | solution.py:132
  349.9 13.5 %collective-permute-start.8 = (bf16[16,1024]{1,0:T(8,128)(2,1)S(1)}, bf16[16,1024]{1,0:T(8,128)(2,1)S(1)}, u32[]{:S(2)}, u32[]{:S(2)}) collective-permute-start(bf16[16,1024]{1,0:T(8,128)(2,1)S(1)} %get-tuple-element.62), channel_id=1, source_target_pairs={{64,0},{128,64},{192,128},{65,1},{129,65},{193,129},{66,2},{130,66... | collective-permute-start | bytes 98312 | tf_op jit(solution)/shard_map/ppermute | solution.py:15
  377.3 91.8 %reduce-scatter.37.cloned.1.call-start = ((), (), s32[]{:S(2)}) async-start(), calls=%async_computation.24 | async-start | bytes 163840 | tf_op jit(solution)/shard_map/reduce_scatter | solution.py:132
  410.0 14.5 %collective-permute-start.9 = (bf16[16,1024]{1,0:T(8,128)(2,1)S(1)}, bf16[16,1024]{1,0:T(8,128)(2,1)S(1)}, u32[]{:S(2)}, u32[]{:S(2)}) collective-permute-start(bf16[16,1024]{1,0:T(8,128)(2,1)S(1)} %get-tuple-element.60), channel_id=1, source_target_pairs={{64,0},{128,64},{192,128},{65,1},{129,65},{193,129},{66,2},{130,66... | collective-permute-start | bytes 98312 | tf_op jit(solution)/shard_map/ppermute | solution.py:15
  438.6 91.5 %reduce-scatter.39.cloned.1.call-start = ((), (), s32[]{:S(2)}) async-start(), calls=%async_computation.25 | async-start | bytes 163840 | tf_op jit(solution)/shard_map/reduce_scatter | solution.py:132
  471.1 14.4 %collective-permute-start.10 = (bf16[16,1024]{1,0:T(8,128)(2,1)S(1)}, bf16[16,1024]{1,0:T(8,128)(2,1)S(1)}, u32[]{:S(2)}, u32[]{:S(2)}) collective-permute-start(bf16[16,1024]{1,0:T(8,128)(2,1)S(1)} %get-tuple-element.58), channel_id=1, source_target_pairs={{64,0},{128,64},{192,128},{65,1},{129,65},{193,129},{66,2},{130,66... | collective-permute-start | bytes 98312 | tf_op jit(solution)/shard_map/ppermute | solution.py:15
  499.5 92.1 %reduce-scatter.41.cloned.1.call-start = ((), (), s32[]{:S(2)}) async-start(), calls=%async_computation.26 | async-start | bytes 163840 | tf_op jit(solution)/shard_map/reduce_scatter | solution.py:132
  532.6 14.4 %collective-permute-start.11 = (bf16[16,1024]{1,0:T(8,128)(2,1)S(1)}, bf16[16,1024]{1,0:T(8,128)(2,1)S(1)}, u32[]{:S(2)}, u32[]{:S(2)}) collective-permute-start(bf16[16,1024]{1,0:T(8,128)(2,1)S(1)} %get-tuple-element.56), channel_id=1, source_target_pairs={{64,0},{128,64},{192,128},{65,1},{129,65},{193,129},{66,2},{130,66... | collective-permute-start | bytes 98312 | tf_op jit(solution)/shard_map/ppermute | solution.py:15
  560.9 92.1 %reduce-scatter.43.cloned.1.call-start = ((), (), s32[]{:S(2)}) async-start(), calls=%async_computation.27 | async-start | bytes 163840 | tf_op jit(solution)/shard_map/reduce_scatter | solution.py:132
  594.0 14.4 %collective-permute-start.12 = (bf16[16,1024]{1,0:T(8,128)(2,1)S(1)}, bf16[16,1024]{1,0:T(8,128)(2,1)S(1)}, u32[]{:S(2)}, u32[]{:S(2)}) collective-permute-start(bf16[16,1024]{1,0:T(8,128)(2,1)S(1)} %get-tuple-element.54), channel_id=1, source_target_pairs={{64,0},{128,64},{192,128},{65,1},{129,65},{193,129},{66,2},{130,66... | collective-permute-start | bytes 98312 | tf_op jit(solution)/shard_map/ppermute | solution.py:15
  622.4 91.2 %reduce-scatter.47.cloned.1.call-start = ((), (), s32[]{:S(2)}) async-start(), calls=%async_computation.29 | async-start | bytes 163840 | tf_op jit(solution)/shard_map/reduce_scatter | solution.py:132
  655.5 13.7 %collective-permute-start.13 = (bf16[16,1024]{1,0:T(8,128)(2,1)S(1)}, bf16[16,1024]{1,0:T(8,128)(2,1)S(1)}, u32[]{:S(2)}, u32[]{:S(2)}) collective-permute-start(bf16[16,1024]{1,0:T(8,128)(2,1)S(1)} %get-tuple-element.52), channel_id=1, source_target_pairs={{64,0},{128,64},{192,128},{65,1},{129,65},{193,129},{66,2},{130,66... | collective-permute-start | bytes 98312 | tf_op jit(solution)/shard_map/ppermute | solution.py:15
  683.2 290.8 %reduce-scatter.51.cloned.1.call-start = ((), (), s32[]{:S(2)}) async-start(), calls=%async_computation.31 | async-start | bytes 532480
  716.3 320.0 %reduce-scatter.49.cloned.1.call-start = ((), (), s32[]{:S(2)}) async-start(), calls=%async_computation.30 | async-start | bytes 2228224
  734.9 369.0 %reduce-scatter.45.cloned.1.call-start = ((), (), s32[]{:S(2)}) async-start(), calls=%async_computation.28 | async-start | bytes 2228224 | tf_op jit(solution)/shard_map/reduce_scatter | solution.py:154
  (60 other events, 1085.7 us)
Sparse Core Ops, SparseCore 0:
  32.5 26.6 reduce-scatter.20
  79.0 27.7 reduce-scatter.22
  126.6 27.6 reduce-scatter.24
  173.8 27.8 reduce-scatter.26
  221.4 27.8 reduce-scatter.28
  268.8 27.9 reduce-scatter.30
  317.1 27.7 reduce-scatter.32
  377.4 30.5 reduce-scatter.34
  438.7 30.3 reduce-scatter.36
  499.6 30.4 reduce-scatter.38
  561.1 30.4 reduce-scatter.40
  622.6 30.4 reduce-scatter.42
  683.3 30.2 reduce-scatter.46
  716.4 257.5 reduce-scatter.50
  976.4 59.8 reduce-scatter.48
  1038.6 65.1 reduce-scatter.44
where the time goes:
time: 1120 us; the launch traced here: 1110 us
  waiting for transfers between devices  712 us (64%)
  blocking collectives  223 us (20%)
  matrix products  48.1 us (4%)
  other arithmetic  44.7 us (4%)
  local copies, waits for them, and re-layouts  36 us (3%)
  starting transfers between devices  32.7 us (3%)
  between operations  15.1 us (1%)
    unnamed x18, waiting for transfers between devices  297 us
    reduce_scatter x7, waiting for transfers between devices, per_device(): lax.psum_scatter(up_term(jnp.int32(0), rows * lax.axis_size('tensor')).as...  190 us
    reduce_scatter x6, waiting for transfers between devices, per_device(): lax.psum_scatter(down_term(jnp.int32(0), rows * lax.axis_size('tensor'))....  154 us
    all_gather x7, blocking collectives, regather(): norm_full = lax.all_gather(norm_rows, 'tensor', axis=0, tiled=True)  76.9 us
    all_gather x7, blocking collectives, per_device(): grad_full = lax.all_gather(grad_rows, 'tensor', axis=0, tiled=True)  76.5 us
    all_gather x6, blocking collectives, per_device(): norm_full = lax.all_gather(norm_rows, 'tensor', axis=0, tiled=True)  69.7 us
    reduce_scatter x1, waiting for transfers between devices, per_device(): lax.psum_scatter(up_grad[None].astype(jnp.bfloat16), 'dp', scatter_dimens...  65.5 us
    ppermute x14, starting transfers between devices, shifted(): lax.ppermute(value, axis, [(source, source + steps) for source in range(i...  31.9 us
  transfers between devices with their start and end apart: 30, of which 22 were waited for; matrix products, arithmetic and copies ran while one was open for 6% of the time, Pallas kernels for 0%

commit v1 on v0

v1 whole, which is shorter than its diff:
```python
import functools
import math

import jax
import jax.numpy as jnp
from jax import lax
from jax.experimental import pallas as pl
from jax.experimental.pallas import tpu as pltpu
from jax.sharding import PartitionSpec as P

MESH = pl.DeviceIdType.MESH
BF16 = jnp.bfloat16
F32 = jnp.float32
EPS = 1e-05
COEF = 0.044715
ROOT = math.sqrt(2.0 / math.pi)
RING = 8


def dot(left, right, dims):
    return lax.dot_general(left, right, ((dims[:1], dims[1:]), ((), ())), preferred_element_type=F32)


def stats(rows):
    centre = rows - jnp.mean(rows, axis=-1, keepdims=True)
    spread = jnp.mean(centre * centre, axis=-1, keepdims=True)
    scale = lax.rsqrt(spread + EPS)
    return centre * scale, scale


def kernel(
    inp, gains, wu_h, wd_h, og,
    up_o, dn_o, gain_o,
    wu, wd, h_full, part_f, send_f, g_full, part_b, send_b,
    normed_s, scale_s, norm_s, slope_s, act_all, pg_all, nc_all, gc_all,
    up_acc, dn_acc, up_send, dn_send, up_in, dn_in,
    gain_acc, g1, g2,
    loc, agf_s, agf_r, rsf_s, rsf_r, agb_s, agb_r, rsb_s, rsb_r,
    act_ss, act_r, nc_ss, nc_r, pg_ss, pg_r, gc_ss, gc_r,
    up_ss, up_r, dn_ss, dn_r, g1_ss, g1_r, g2_ss, g2_r,
    *, sections, n_y,
):
    micro, rows, width = inp.shape
    full = 4 * rows
    span = width // n_y
    share = span // 4
    s = lax.axis_index("section")
    p = lax.axis_index("dp")
    t = lax.axis_index("tensor")
    core = p % 2
    z_lo = (p // 2) % 2
    y = p // 4
    z = 2 * t + z_lo
    e = 2 * z_lo - 1

    def place(section, y_at, z_at, core_at):
        z_at = (z_at + 2 * RING) % RING
        return (section, (y_at * 2 + z_at % 2) * 2 + core_at, z_at // 2)

    def send(src, dst, ssem, rsem, device):
        pltpu.make_async_remote_copy(
            src_ref=src, dst_ref=dst, send_sem=ssem, recv_sem=rsem,
            device_id=device, device_id_type=MESH,
        ).start()

    def wait(region, sem):
        pltpu.make_async_copy(region, region, sem).wait()

    load_wu = pltpu.make_async_copy(wu_h.at[0], wu, loc.at[0])
    load_wd = pltpu.make_async_copy(wd_h.at[0], wd, loc.at[1])
    first = s == 0
    last = s == sections - 1

    @pl.when(first)
    def _():
        pltpu.make_async_copy(inp, h_full.at[:, pl.ds(0, rows)], loc.at[2]).start()

    @pl.when(last)
    def _():
        pltpu.make_async_copy(og, g_full.at[:, pl.ds(0, rows)], loc.at[3]).start()

    load_wu.start()
    load_wd.start()

    barrier = pltpu.get_barrier_semaphore()

    def greet(device):
        pl.semaphore_signal(barrier, inc=1, device_id=device, device_id_type=MESH)

    for dz in range(RING):
        for dc in range(2):
            if dz or dc:
                greet(place(s, y, z + dz, (core + dc) % 2))
    for dy in range(1, n_y):
        greet(place(s, (y + dy) % n_y, z, core))
    for step in (-2, 0, 1, 2, 3):
        @pl.when(jnp.logical_not(first))
        def _():
            greet(place(s - 1, y, z + e * step, core))

        @pl.when(jnp.logical_not(last))
        def _():
            greet(place(s + 1, y, z + e * step, core))

    within = 2 * RING - 1 + n_y - 1
    edge = jnp.logical_or(first, last)

    @pl.when(edge)
    def _():
        pl.semaphore_wait(barrier, within + 5 * (sections > 1))

    @pl.when(jnp.logical_not(edge))
    def _():
        pl.semaphore_wait(barrier, within + 10)

    peers = ((1, 1), (2, -2), (3, 3))

    def gather(buf, m, ssem, rsem):
        for slot, step in peers:
            send(
                buf.at[m, pl.ds(0, rows)], buf.at[m, pl.ds(slot * rows, rows)],
                ssem.at[m], rsem.at[m], place(s, y, z + e * step, core),
            )

    def scatter(src, dst, m, ssem, rsem, section):
        for slot in range(4):
            send(
                src.at[m, pl.ds(slot * rows, rows)], dst.at[m, slot],
                ssem.at[m], rsem.at[m], place(section, y, z + e * slot, core),
            )

    def to_y(buf, m, ssem, rsem):
        for dy in range(1, n_y):
            send(buf.at[m, 0], buf.at[m, dy], ssem.at[m], rsem.at[m], place(s, (y + dy) % n_y, z, core))

    def cols_to_y(src, buf, m, ssem, rsem):
        for dy in range(1, n_y):
            y_at = (y + dy) % n_y
            send(
                src.at[m, :, pl.ds(pl.multiple_of(y_at * span, span), span)], buf.at[m, dy],
                ssem.at[m], rsem.at[m], place(s, y_at, z, core),
            )

    own_cols = pl.ds(pl.multiple_of(y * span, span), span)
    gain_row = gains[...]

    def rows_f(m):
        @pl.when(jnp.logical_not(first))
        def _():
            wait(part_f.at[m], rsf_r.at[m])
            total = part_f[m, 0].astype(F32)
            for slot in range(1, 4):
                total = total + part_f[m, slot].astype(F32)
            h_full[m, pl.ds(0, rows)] = total.astype(BF16)

        gather(h_full, m, agf_s, agf_r)

    def step_f(m):
        wait(h_full.at[m, pl.ds(rows, 3 * rows)], agf_r.at[m])
        hidden = h_full[m].astype(F32)
        normed, scale = stats(hidden)
        norm = (normed * gain_row).astype(BF16)
        preact = dot(norm, wu[...], (1, 0))
        inner = ROOT * (preact + COEF * preact * preact * preact)
        tangent = jnp.tanh(inner)
        act = (0.5 * preact * (1.0 + tangent)).astype(BF16)
        act_all[m, 0] = act

        @pl.when(jnp.logical_not(last))
        def _():
            mixed = dot(act, wd[...], (1, 0))
            send_f[m, pl.ds(0, rows)] = (mixed[:rows] + hidden[:rows]).astype(BF16)
            send_f[m, pl.ds(rows, 3 * rows)] = mixed[rows:].astype(BF16)
            scatter(send_f, part_f, m, rsf_s, rsf_r, s + 1)

        slope_s[m] = 0.5 * (1.0 + tangent) + 0.5 * preact * (1.0 - tangent * tangent) * ROOT * (
            1.0 + 3.0 * COEF * preact * preact
        )
        normed_s[m] = normed
        scale_s[m] = jnp.broadcast_to(scale, (full, 128))
        norm_s[m] = norm
        nc_all[m, 0] = norm_s[m, :, own_cols]
        cols_to_y(norm_s, nc_all, m, nc_ss, nc_r)
        to_y(act_all, m, act_ss, act_r)

    @pl.when(first)
    def _():
        pltpu.make_async_copy(inp, h_full.at[:, pl.ds(0, rows)], loc.at[2]).wait()

    rows_f(0)

    @pl.when(last)
    def _():
        pltpu.make_async_copy(og, g_full.at[:, pl.ds(0, rows)], loc.at[3]).wait()
        for m in range(micro):
            gather(g_full, m, agb_s, agb_r)

    load_wu.wait()
    load_wd.wait()

    def loop_f(m, carry):
        @pl.when(m < micro - 1)
        def _():
            rows_f(m + 1)

        step_f(m)
        return carry

    lax.fori_loop(0, micro, loop_f, 0)

    gain_acc[...] = jnp.zeros_like(gain_acc)

    def rows_b(m):
        @pl.when(jnp.logical_not(last))
        def _():
            wait(part_b.at[m], rsb_r.at[m])
            total = part_b[m, 0].astype(F32)
            for slot in range(1, 4):
                total = total + part_b[m, slot].astype(F32)
            g_full[m, pl.ds(0, rows)] = total.astype(BF16)
            gather(g_full, m, agb_s, agb_r)

    def step_b(m):
        wait(g_full.at[m, pl.ds(rows, 3 * rows)], agb_r.at[m])
        grad = g_full[m]
        down_grad = dot(grad, wd[...], (1, 1))
        pg = (down_grad * slope_s[m]).astype(BF16)
        pg_all[m, 0] = pg
        to_y(pg_all, m, pg_ss, pg_r)
        norm_grad = dot(pg, wu[...], (1, 1))
        normed = normed_s[m]

        @pl.when(jnp.logical_not(first))
        def _():
            scaled = norm_grad * gain_row
            back = scale_s[m][:, :1] * (
                scaled
                - jnp.mean(scaled, axis=-1, keepdims=True)
                - normed * jnp.mean(scaled * normed, axis=-1, keepdims=True)
            )
            send_b[m, pl.ds(0, rows)] = (back[:rows] + grad[:rows].astype(F32)).astype(BF16)
            send_b[m, pl.ds(rows, 3 * rows)] = back[rows:].astype(BF16)
            scatter(send_b, part_b, m, rsb_s, rsb_r, s - 1)

        terms = norm_grad * normed
        total = terms[0:8]
        for at in range(8, full, 8):
            total = total + terms[at:at + 8]
        gain_acc[...] += total
        gc_all[m, 0] = g_full[m, :, own_cols]
        cols_to_y(g_full, gc_all, m, gc_ss, gc_r)

    rows_b(0)

    def loop_b(m, carry):
        @pl.when(m < micro - 1)
        def _():
            rows_b(m + 1)

        step_b(m)
        return carry

    lax.fori_loop(0, micro, loop_b, 0)

    total = jnp.sum(gain_acc[...], axis=0, keepdims=True)
    lines = width // 128
    for line in range(lines):
        g1[0, line:line + 1] = total[:, line * 128:(line + 1) * 128]
    for dy in range(1, n_y):
        send(g1.at[0], g1.at[dy], g1_ss.at[0], g1_r.at[0], place(s, (y + dy) % n_y, z, core))

    dn_acc[...] = jnp.zeros_like(dn_acc)
    up_acc[...] = jnp.zeros_like(up_acc)

    def down_part(m, carry):
        if n_y > 1:
            wait(act_all.at[m, pl.ds(1, n_y - 1)], act_r.at[m])
            wait(gc_all.at[m, pl.ds(1, n_y - 1)], gc_r.at[m])
        cols = gc_all[m].reshape(n_y * full, span)
        dn_acc[...] += dot(cols, act_all[m].reshape(n_y * full, -1), (0, 0))
        return carry

    def up_part(m, carry):
        if n_y > 1:
            wait(nc_all.at[m, pl.ds(1, n_y - 1)], nc_r.at[m])
            wait(pg_all.at[m, pl.ds(1, n_y - 1)], pg_r.at[m])
        cols = nc_all[m].reshape(n_y * full, span)
        up_acc[...] += dot(cols, pg_all[m].reshape(n_y * full, -1), (0, 0))
        return carry

    def exchange(acc, out, into, ssem, rsem):
        out[...] = acc[...].astype(BF16)
        for rel in range(1, 4):
            z_lo_at = (z_lo + rel // 2) % 2
            core_at = (core + rel % 2) % 2
            block = z_lo_at * 2 + core_at
            send(
                out.at[pl.ds(pl.multiple_of(block * share, share), share)], into.at[rel - 1],
                ssem.at[0], rsem.at[0], place(s, y, 2 * t + z_lo_at, core_at),
            )

    own_block = pl.ds(pl.multiple_of((z_lo * 2 + core) * share, share), share)

    def finish(acc, into):
        total = acc[own_block]
        for rel in range(3):
            total = total + into[rel].astype(F32)
        return total

    lax.fori_loop(0, micro - 1, up_part, 0)
    lax.fori_loop(0, micro, down_part, 0)
    exchange(dn_acc, dn_send, dn_in, dn_ss, dn_r)
    up_part(micro - 1, 0)
    exchange(up_acc, up_send, up_in, up_ss, up_r)

    if n_y > 1:
        wait(g1.at[pl.ds(1, n_y - 1)], g1_r.at[0])
    total = g1[0]
    for dy in range(1, n_y):
        total = total + g1[dy]
    g2[0] = total
    for dz in range(RING):
        for dc in range(2):
            if dz or dc:
                send(
                    g2.at[0], g2.at[dz * 2 + dc], g2_ss.at[0], g2_r.at[0],
                    place(s, y, z + dz, (core + dc) % 2),
                )

    wait(dn_in, dn_r.at[0])
    dn_o[0] = finish(dn_acc, dn_in).T

    wait(g2.at[pl.ds(1, 2 * RING - 1)], g2_r.at[0])
    total = g2[0]
    for peer in range(1, 2 * RING):
        total = total + g2[peer]
    per = gain_o.shape[1]
    fold = 128 // per
    index = p * 4 + t
    line_at = lax.broadcasted_iota(jnp.int32, total.shape, 0)
    line = jnp.sum(jnp.where(line_at == index // fold, total, 0.0), axis=0, keepdims=True)
    piece = jnp.zeros((1, per), F32)
    for at in range(fold):
        piece = piece + jnp.where(index % fold == at, line[:, at * per:(at + 1) * per], 0.0)
    gain_o[...] = piece

    wait(up_in, up_r.at[0])
    up_o[0] = finish(up_acc, up_in)

    def drain(m, carry):
        wait(h_full.at[m, pl.ds(rows, 3 * rows)], agf_s.at[m])
        wait(g_full.at[m, pl.ds(rows, 3 * rows)], agb_s.at[m])

        @pl.when(jnp.logical_not(last))
        def _():
            wait(part_f.at[m], rsf_s.at[m])

        @pl.when(jnp.logical_not(first))
        def _():
            wait(part_b.at[m], rsb_s.at[m])

        if n_y > 1:
            wait(act_all.at[m, pl.ds(1, n_y - 1)], act_ss.at[m])
            wait(pg_all.at[m, pl.ds(1, n_y - 1)], pg_ss.at[m])
            wait(nc_all.at[m, pl.ds(1, n_y - 1)], nc_ss.at[m])
            wait(gc_all.at[m, pl.ds(1, n_y - 1)], gc_ss.at[m])
        return carry

    lax.fori_loop(0, micro, drain, 0)
    if n_y > 1:
        wait(g1.at[pl.ds(1, n_y - 1)], g1_ss.at[0])
    wait(g2.at[pl.ds(1, 2 * RING - 1)], g2_ss.at[0])
    wait(dn_in, dn_ss.at[0])
    wait(up_in, up_ss.at[0])


def solution(mesh):
    sections, n_dp, n_tensor = (mesh.shape[axis] for axis in ("section", "dp", "tensor"))
    n_y = n_dp // 4

    def per_device(inputs, gains, w_up, w_down, out_grad):
        micro, rows, width = inputs.shape
        hid = w_up.shape[2]
        full = 4 * rows
        span = width // n_y
        share = span // 4
        per = width // (n_dp * n_tensor)
        any_space = pl.BlockSpec(memory_space=pl.ANY)
        vmem = pl.BlockSpec(memory_space=pltpu.VMEM)
        dma = pltpu.SemaphoreType.DMA
        many, one = dma((micro,)), dma((1,))
        return pl.pallas_call(
            functools.partial(kernel, sections=sections, n_y=n_y),
            out_shape=(
                jax.ShapeDtypeStruct((1, share, hid), F32),
                jax.ShapeDtypeStruct((1, hid, share), F32),
                jax.ShapeDtypeStruct((1, per), F32),
            ),
            in_specs=[any_space, vmem, any_space, any_space, any_space],
            out_specs=(vmem, vmem, vmem),
            scratch_shapes=[
                pltpu.VMEM((width, hid), BF16),
                pltpu.VMEM((hid, width), BF16),
                pltpu.VMEM((micro, full, width), BF16),
                pltpu.VMEM((micro, 4, rows, width), BF16),
                pltpu.VMEM((micro, full, width), BF16),
                pltpu.VMEM((micro, full, width), BF16),
                pltpu.VMEM((micro, 4, rows, width), BF16),
                pltpu.VMEM((micro, full, width), BF16),
                pltpu.VMEM((micro, full, width), F32),
                pltpu.VMEM((micro, full, 128), F32),
                pltpu.VMEM((micro, full, width), BF16),
                pltpu.VMEM((micro, full, hid), F32),
                pltpu.VMEM((micro, n_y, full, hid), BF16),
                pltpu.VMEM((micro, n_y, full, hid), BF16),
                pltpu.VMEM((micro, n_y, full, span), BF16),
                pltpu.VMEM((micro, n_y, full, span), BF16),
                pltpu.VMEM((span, hid), F32),
                pltpu.VMEM((span, hid), F32),
                pltpu.VMEM((span, hid), BF16),
                pltpu.VMEM((span, hid), BF16),
                pltpu.VMEM((3, share, hid), BF16),
                pltpu.VMEM((3, share, hid), BF16),
                pltpu.VMEM((8, width), F32),
                pltpu.VMEM((n_y, width // 128, 128), F32),
                pltpu.VMEM((2 * RING, width // 128, 128), F32),
                dma((4,)),
            ] + [many] * 16 + [one] * 8,
            compiler_params=pltpu.CompilerParams(
                collective_id=0, has_side_effects=True, vmem_limit_bytes=50 * 1024 * 1024
            ),
        )(inputs, gains, w_up, w_down, out_grad)

    return jax.shard_map(
        per_device,
        mesh=mesh,
        in_specs=(
            P(None, ("dp", "tensor"), None),
            P("section", None),
            P("section", None, "tensor"),
            P("section", "tensor", None),
            P(None, ("dp", "tensor"), None),
        ),
        out_specs=(
            P("section", "dp", "tensor"),
            P("section", "tensor", "dp"),
            P("section", ("dp", "tensor")),
        ),
        check_vma=False,
    )
```

time: 1120 us -> 164 us (0.15)
  waiting for transfers between devices: 712 us -> 0 us
  blocking collectives: 223 us -> 0 us
  Pallas kernels: 0 us -> 156 us
  matrix products: 48.1 us -> 0 us
  other arithmetic: 44.7 us -> 0 us
  starting transfers between devices: 32.7 us -> 0 us
  local copies, waits for them, and re-layouts: 36 us -> 6.18 us
  between operations: 15.1 us -> 0.65 us
    reduce_scatter x14 -> x0, waiting for transfers between devices: 410 us -> none  [the longest x7 190 us: per_device(): lax.psum_scatter(up_term(jnp.int32(0), rows * lax.axis_size('tensor')).as...]
    unnamed x18 -> x0, waiting for transfers between devices: 297 us -> none
    all_gather x20 -> x0, blocking collectives: 223 us -> none  [the longest x7 76.9 us: regather(): norm_full = lax.all_gather(norm_rows, 'tensor', axis=0, tiled=True)]
    pallas_call x0 -> x1, Pallas kernels: none -> 156 us  [per_device(): pl.pallas_call(functools.partial(kernel, sections=sections, n_y=n_y), out...]
    dot_general x29 -> x0, matrix products: 48.1 us -> none  [the longest x6 18.9 us: down_term(): return jnp.dot(activated, down_local, preferred_element_type=jnp.float32)]
    ppermute x14 -> x0, starting transfers between devices: 31.9 us -> none  [shifted(): lax.ppermute(value, axis, [(source, source + steps) for source in range(i...]
    dynamic_slice x30 -> x0, local copies, waits for them, and re-layouts: 15.3 us -> none  [pick(): return lax.dynamic_index_in_dim(stack, slot, 0, keepdims=False)]
    unnamed x115 -> x10, local copies, waits for them, and re-layouts: 20.5 us -> 5.29 us
  transfers between devices with their start and end apart: 30 -> 0, of which waited for: 22 -> 0; matrix products, arithmetic and copies ran while one was open for 6% -> 0% of each run, Pallas kernels for 0% -> 0%
where the time goes in v1:
time: 164 us; the launch traced here: 163 us
  Pallas kernels  156 us (95%)
  local copies, waits for them, and re-layouts  6.18 us (4%)
    pallas_call x1, Pallas kernels, per_device(): pl.pallas_call(functools.partial(kernel, sections=sections, n_y=n_y), out...  156 us
    unnamed x10, local copies, waits for them, and re-layouts  5.29 us

profile of v1, /device:TPU:1, one launch (start us, length us, event | category | flops | bytes accessed | tf_op | source)
XLA Modules:
  0.0 163.0 jit_solution(15330609086458234860)
XLA Ops:
  0.6 0.0 copy-start
  0.6 1.6 copy-done
  2.2 0.0 copy-start.1
  2.2 0.9 copy-done.1
  3.1 0.0 copy-start.2
  3.1 0.9 copy-done.2
  4.0 0.0 copy-start.3
  4.0 0.7 copy-done.3
  4.7 156.2 %shard_map.76 = (f32[1,64,1024]{2,1,0:T(8,128)S(1)}, f32[1,1024,64]{2,1,0:T(8,128)S(1)}, f32[1,16]{1,0:T(1,128)S(1)}) custom-call(bf16[4,16,1024]{2,1,0:T(8,128)(2,1)S(1)} %copy-done.1, f32[1,1024]{1,0:T(1,128)S(1)} %copy-done.3, bf16[1,1024,1024]{2,1,0:T(8,128)(2,1)S(1)} %copy-done, bf16[1,1024,1024]{2,1,0:T(8,128)(2,1)} %wd_h.1, ...), custom_call_target="tpu_custom_call" | custom-call | tf_op jit(solution)/shard_map/pallas_call | solution.py:392
  160.9 0.9 copy.8
  161.8 0.7 copy.11
  162.5 0.5 copy.12
Async XLA Ops:
  0.6 1.6 copy-start
  2.2 0.9 copy-start.1
  3.1 0.9 copy-start.2
  4.0 0.7 copy-start.3

commit v2 on v1

--- a/solution.py
+++ b/solution.py
@@ -29,15 +29,15 @@
 
 
 def kernel(
-    inp, gains, wu_h, wd_h, og,
+    inp, gains_h, wu_h, wd_h, og,
     up_o, dn_o, gain_o,
     wu, wd, h_full, part_f, send_f, g_full, part_b, send_b,
-    normed_s, scale_s, norm_s, slope_s, act_all, pg_all, nc_all, gc_all,
-    up_acc, dn_acc, up_send, dn_send, up_in, dn_in,
+    gains, normed_s, scale_s, norm_s, slope_s, act_all, pg_all, nc_all, gc_all,
+    wu_t, wd_t, up_acc, dn_acc, up_buf, dn_buf,
     gain_acc, g1, g2,
     loc, agf_s, agf_r, rsf_s, rsf_r, agb_s, agb_r, rsb_s, rsb_r,
     act_ss, act_r, nc_ss, nc_r, pg_ss, pg_r, gc_ss, gc_r,
-    up_ss, up_r, dn_ss, dn_r, g1_ss, g1_r, g2_ss, g2_r,
+    up_ss, up_r, dn_ss, dn_r, up2_ss, up2_r, dn2_ss, dn2_r, g1_ss, g1_r, g2_ss, g2_r,
     *, sections, n_y,
 ):
     micro, rows, width = inp.shape
@@ -79,6 +79,8 @@
     def _():
         pltpu.make_async_copy(og, g_full.at[:, pl.ds(0, rows)], loc.at[3]).start()
 
+    load_gains = pltpu.make_async_copy(gains_h, gains, loc.at[4])
+    load_gains.start()
     load_wu.start()
     load_wd.start()
 
@@ -113,7 +115,7 @@
     def _():
         pl.semaphore_wait(barrier, within + 10)
 
-    peers = ((1, 1), (2, -2), (3, 3))
+    peers = ((3, 3), (2, -2), (1, 1))
 
     def gather(buf, m, ssem, rsem):
         for slot, step in peers:
@@ -123,7 +125,7 @@
             )
 
     def scatter(src, dst, m, ssem, rsem, section):
-        for slot in range(4):
+        for slot in (3, 2, 1, 0):
             send(
                 src.at[m, pl.ds(slot * rows, rows)], dst.at[m, slot],
                 ssem.at[m], rsem.at[m], place(section, y, z + e * slot, core),
@@ -142,7 +144,6 @@
             )
 
     own_cols = pl.ds(pl.multiple_of(y * span, span), span)
-    gain_row = gains[...]
 
     def rows_f(m):
         @pl.when(jnp.logical_not(first))
@@ -187,7 +188,9 @@
     def _():
         pltpu.make_async_copy(inp, h_full.at[:, pl.ds(0, rows)], loc.at[2]).wait()
 
-    rows_f(0)
+    @pl.when(jnp.logical_not(last))
+    def _():
+        rows_f(0)
 
     @pl.when(last)
     def _():
@@ -195,18 +198,10 @@
         for m in range(micro):
             gather(g_full, m, agb_s, agb_r)
 
+    load_gains.wait()
     load_wu.wait()
     load_wd.wait()
-
-    def loop_f(m, carry):
-        @pl.when(m < micro - 1)
-        def _():
-            rows_f(m + 1)
-
-        step_f(m)
-        return carry
-
-    lax.fori_loop(0, micro, loop_f, 0)
+    gain_row = gains[...]
 
     gain_acc[...] = jnp.zeros_like(gain_acc)
 
@@ -223,11 +218,13 @@
     def step_b(m):
         wait(g_full.at[m, pl.ds(rows, 3 * rows)], agb_r.at[m])
         grad = g_full[m]
-        down_grad = dot(grad, wd[...], (1, 1))
+        down_grad = dot(grad, wd_t[...], (1, 0))
         pg = (down_grad * slope_s[m]).astype(BF16)
         pg_all[m, 0] = pg
         to_y(pg_all, m, pg_ss, pg_r)
-        norm_grad = dot(pg, wu[...], (1, 1))
+        gc_all[m, 0] = g_full[m, :, own_cols]
+        cols_to_y(g_full, gc_all, m, gc_ss, gc_r)
+        norm_grad = dot(pg, wu_t[...], (1, 0))
         normed = normed_s[m]
 
         @pl.when(jnp.logical_not(first))
@@ -247,20 +244,51 @@
         for at in range(8, full, 8):
             total = total + terms[at:at + 8]
         gain_acc[...] += total
-        gc_all[m, 0] = g_full[m, :, own_cols]
-        cols_to_y(g_full, gc_all, m, gc_ss, gc_r)
-
-    rows_b(0)
-
-    def loop_b(m, carry):
-        @pl.when(m < micro - 1)
-        def _():
-            rows_b(m + 1)
-
-        step_b(m)
+
+    def transpose(weight, into):
+        step = 256
+        count = weight.shape[0] // step
+
+        def piece(at, carry):
+            part = pl.ds(pl.multiple_of(at * step, step), step)
+            into[:, part] = weight[part].T
+            return carry
+
+        lax.fori_loop(0, count, piece, 0)
+
+    @pl.when(jnp.logical_not(first))
+    def _():
+        transpose(wd, wd_t)
+        transpose(wu, wu_t)
+
+    turn = s // (sections - 1)
+
+    def step(i, carry):
+        back = turn * (i % 2) + (1 - turn) * (i // micro)
+        m = turn * (i // 2) + (1 - turn) * (i % micro)
+        ahead = m + 1 - turn
+
+        @pl.when(back == 0)
+        def _():
+            @pl.when(ahead < micro)
+            def _():
+                rows_f(ahead)
+
+            step_f(m)
+
+        @pl.when(back == 1)
+        def _():
+            @pl.when(jnp.logical_and(first, m == 0))
+            def _():
+                transpose(wd, wd_t)
+                transpose(wu, wu_t)
+
+            rows_b(m)
+            step_b(m)
+
         return carry
 
-    lax.fori_loop(0, micro, loop_b, 0)
+    lax.fori_loop(0, 2 * micro, step, 0)
 
     total = jnp.sum(gain_acc[...], axis=0, keepdims=True)
     lines = width // 128
@@ -288,30 +316,29 @@
         up_acc[...] += dot(cols, pg_all[m].reshape(n_y * full, -1), (0, 0))
         return carry
 
-    def exchange(acc, out, into, ssem, rsem):
-        out[...] = acc[...].astype(BF16)
-        for rel in range(1, 4):
-            z_lo_at = (z_lo + rel // 2) % 2
-            core_at = (core + rel % 2) % 2
-            block = z_lo_at * 2 + core_at
-            send(
-                out.at[pl.ds(pl.multiple_of(block * share, share), share)], into.at[rel - 1],
-                ssem.at[0], rsem.at[0], place(s, y, 2 * t + z_lo_at, core_at),
-            )
-
-    own_block = pl.ds(pl.multiple_of((z_lo * 2 + core) * share, share), share)
-
-    def finish(acc, into):
-        total = acc[own_block]
-        for rel in range(3):
-            total = total + into[rel].astype(F32)
-        return total
+    other = 1 - core
+
+    def block(z_lo_at, core_at):
+        return pl.ds(pl.multiple_of((z_lo_at * 2 + core_at) * share, share), share)
+
+    def to_core(acc, buf, ssem, rsem):
+        for z_lo_at in range(2):
+            buf[z_lo_at] = acc[block(z_lo_at, other)].astype(BF16)
+        send(buf.at[pl.ds(0, 2)], buf.at[pl.ds(2, 2)], ssem.at[0], rsem.at[0], place(s, y, z, other))
+
+    def to_pair(acc, buf, rsem, ssem2, rsem2):
+        wait(buf.at[pl.ds(2, 2)], rsem.at[0])
+        away = 1 - z_lo
+        buf[4] = (acc[block(away, core)] + buf[2 + away].astype(F32)).astype(BF16)
+        send(buf.at[4], buf.at[5], ssem2.at[0], rsem2.at[0], place(s, y, 2 * t + away, core))
+
+    def finish(acc, buf, rsem2):
+        wait(buf.at[5], rsem2.at[0])
+        return acc[block(z_lo, core)] + buf[2 + z_lo].astype(F32) + buf[5].astype(F32)
 
     lax.fori_loop(0, micro - 1, up_part, 0)
     lax.fori_loop(0, micro, down_part, 0)
-    exchange(dn_acc, dn_send, dn_in, dn_ss, dn_r)
-    up_part(micro - 1, 0)
-    exchange(up_acc, up_send, up_in, up_ss, up_r)
+    to_core(dn_acc, dn_buf, dn_ss, dn_r)
 
     if n_y > 1:
         wait(g1.at[pl.ds(1, n_y - 1)], g1_r.at[0])
@@ -327,8 +354,11 @@
                     place(s, y, z + dz, (core + dc) % 2),
                 )
 
-    wait(dn_in, dn_r.at[0])
-    dn_o[0] = finish(dn_acc, dn_in).T
+    to_pair(dn_acc, dn_buf, dn_r, dn2_ss, dn2_r)
+    up_part(micro - 1, 0)
+    to_core(up_acc, up_buf, up_ss, up_r)
+    to_pair(up_acc, up_buf, up_r, up2_ss, up2_r)
+    dn_o[0] = finish(dn_acc, dn_buf, dn2_r)
 
     wait(g2.at[pl.ds(1, 2 * RING - 1)], g2_r.at[0])
     total = g2[0]
@@ -344,8 +374,7 @@
         piece = piece + jnp.where(index % fold == at, line[:, at * per:(at + 1) * per], 0.0)
     gain_o[...] = piece
 
-    wait(up_in, up_r.at[0])
-    up_o[0] = finish(up_acc, up_in)
+    up_o[0] = finish(up_acc, up_buf, up2_r)
 
     def drain(m, carry):
         wait(h_full.at[m, pl.ds(rows, 3 * rows)], agf_s.at[m])
@@ -370,8 +399,10 @@
     if n_y > 1:
         wait(g1.at[pl.ds(1, n_y - 1)], g1_ss.at[0])
     wait(g2.at[pl.ds(1, 2 * RING - 1)], g2_ss.at[0])
-    wait(dn_in, dn_ss.at[0])
-    wait(up_in, up_ss.at[0])
+    wait(dn_buf.at[pl.ds(0, 2)], dn_ss.at[0])
+    wait(up_buf.at[pl.ds(0, 2)], up_ss.at[0])
+    wait(dn_buf.at[4], dn2_ss.at[0])
+    wait(up_buf.at[4], up2_ss.at[0])
 
 
 def solution(mesh):
@@ -385,18 +416,18 @@
         span = width // n_y
         share = span // 4
         per = width // (n_dp * n_tensor)
-        any_space = pl.BlockSpec(memory_space=pl.ANY)
+        hbm = pl.BlockSpec(memory_space=pltpu.HBM)
         vmem = pl.BlockSpec(memory_space=pltpu.VMEM)
         dma = pltpu.SemaphoreType.DMA
         many, one = dma((micro,)), dma((1,))
-        return pl.pallas_call(
+        up, down, gain = pl.pallas_call(
             functools.partial(kernel, sections=sections, n_y=n_y),
             out_shape=(
                 jax.ShapeDtypeStruct((1, share, hid), F32),
-                jax.ShapeDtypeStruct((1, hid, share), F32),
+                jax.ShapeDtypeStruct((1, share, hid), F32),
                 jax.ShapeDtypeStruct((1, per), F32),
             ),
-            in_specs=[any_space, vmem, any_space, any_space, any_space],
+            in_specs=[hbm] * 5,
             out_specs=(vmem, vmem, vmem),
             scratch_shapes=[
                 pltpu.VMEM((width, hid), BF16),
@@ -407,6 +438,7 @@
                 pltpu.VMEM((micro, full, width), BF16),
                 pltpu.VMEM((micro, 4, rows, width), BF16),
                 pltpu.VMEM((micro, full, width), BF16),
+                pltpu.VMEM((1, width), F32),
                 pltpu.VMEM((micro, full, width), F32),
                 pltpu.VMEM((micro, full, 128), F32),
                 pltpu.VMEM((micro, full, width), BF16),
@@ -415,21 +447,22 @@
                 pltpu.VMEM((micro, n_y, full, hid), BF16),
                 pltpu.VMEM((micro, n_y, full, span), BF16),
                 pltpu.VMEM((micro, n_y, full, span), BF16),
+                pltpu.VMEM((hid, width), BF16),
+                pltpu.VMEM((width, hid), BF16),
                 pltpu.VMEM((span, hid), F32),
                 pltpu.VMEM((span, hid), F32),
-                pltpu.VMEM((span, hid), BF16),
-                pltpu.VMEM((span, hid), BF16),
-                pltpu.VMEM((3, share, hid), BF16),
-                pltpu.VMEM((3, share, hid), BF16),
+                pltpu.VMEM((6, share, hid), BF16),
+                pltpu.VMEM((6, share, hid), BF16),
                 pltpu.VMEM((8, width), F32),
                 pltpu.VMEM((n_y, width // 128, 128), F32),
                 pltpu.VMEM((2 * RING, width // 128, 128), F32),
-                dma((4,)),
-            ] + [many] * 16 + [one] * 8,
+                dma((5,)),
+            ] + [many] * 16 + [one] * 12,
             compiler_params=pltpu.CompilerParams(
-                collective_id=0, has_side_effects=True, vmem_limit_bytes=50 * 1024 * 1024
+                collective_id=0, has_side_effects=True, vmem_limit_bytes=63 * 1024 * 1024
             ),
         )(inputs, gains, w_up, w_down, out_grad)
+        return up, jnp.swapaxes(down, 1, 2), gain
 
     return jax.shard_map(
         per_device,

time: 164 us -> 144 us (0.88)
  Pallas kernels: 156 us -> 139 us
  local copies, waits for them, and re-layouts: 6.18 us -> 4.45 us
    pallas_call x1, Pallas kernels: 156 us -> 139 us  [per_device(): pl.pallas_call(functools.partial(kernel, sections=sections, n_y=n_y), out...]
    unnamed x10 -> x3, local copies, waits for them, and re-layouts: 5.29 us -> 4.45 us
where the time goes in v2:
time: 144 us
  Pallas kernels  139 us (97%)
  local copies, waits for them, and re-layouts  4.45 us (3%)
    pallas_call x1, Pallas kernels, per_device(): pl.pallas_call(functools.partial(kernel, sections=sections, n_y=n_y), out...  139 us
    unnamed x3, local copies, waits for them, and re-layouts  4.45 us

profile of v2, /device:TPU:1, one launch (start us, length us, event | category | flops | bytes accessed | tf_op | source)
XLA Modules:
  0.0 143.9 jit_solution(13812874001689686082)
XLA Ops:
  0.6 138.8 %shard_map.76 = (f32[1,64,1024]{2,1,0:T(8,128)}, f32[1,64,1024]{2,1,0:T(8,128)}, f32[1,16]{1,0:T(1,128)}) custom-call(bf16[4,16,1024]{2,1,0:T(8,128)(2,1)} %inp.1, f32[1,1024]{1,0:T(1,128)} %gains_h.1, bf16[1,1024,1024]{2,1,0:T(8,128)(2,1)} %wu_h.1, bf16[1,1024,1024]{2,1,0:T(8,128)(2,1)} %wd_h.1, bf16[4,16,1024]{2,1,0:T(8,128)(2,1)} %og.1), custom_call_target="tpu_custom_call" | custom-call | tf_op jit(solution)/shard_map/pallas_call | solution.py:423
  139.4 1.7 %copy.11 = f32[1,64,1024]{2,1,0:T(8,128)} copy(f32[1,64,1024]{2,1,0:T(8,128)} %get-tuple-element.12) | data formatting | bytes 524288
  141.1 1.7 %copy.12 = f32[1,1024,64]{1,2,0:T(8,128)} copy(f32[1,1024,64]{1,2,0:T(8,128)} %bitcast.1) | data formatting | bytes 524288
  142.7 1.1 copy.13

commit v3 on v2

--- a/solution.py
+++ b/solution.py
@@ -31,11 +31,11 @@
 def kernel(
     inp, gains_h, wu_h, wd_h, og,
     up_o, dn_o, gain_o,
-    wu, wd, h_full, part_f, send_f, g_full, part_b, send_b,
+    wu, wd, own, h_full, part_f, sum_f, send_f, g_full, part_b, sum_b, send_b,
     gains, normed_s, scale_s, norm_s, slope_s, act_all, pg_all, nc_all, gc_all,
     wu_t, wd_t, up_acc, dn_acc, up_buf, dn_buf,
     gain_acc, g1, g2,
-    loc, agf_s, agf_r, rsf_s, rsf_r, agb_s, agb_r, rsb_s, rsb_r,
+    loc, own_s, agf_s, agf_r, rsf_s, rsf_r, agb_s, agb_r, rsb_s, rsb_r,
     act_ss, act_r, nc_ss, nc_r, pg_ss, pg_r, gc_ss, gc_r,
     up_ss, up_r, dn_ss, dn_r, up2_ss, up2_r, dn2_ss, dn2_r, g1_ss, g1_r, g2_ss, g2_r,
     *, sections, n_y,
@@ -71,14 +71,10 @@
     first = s == 0
     last = s == sections - 1
 
-    @pl.when(first)
-    def _():
-        pltpu.make_async_copy(inp, h_full.at[:, pl.ds(0, rows)], loc.at[2]).start()
-
-    @pl.when(last)
-    def _():
-        pltpu.make_async_copy(og, g_full.at[:, pl.ds(0, rows)], loc.at[3]).start()
-
+    load_in = pltpu.make_async_copy(inp.at[s], own.at[0], loc.at[2])
+    load_og = pltpu.make_async_copy(og.at[s], own.at[1], loc.at[3])
+    load_in.start()
+    load_og.start()
     load_gains = pltpu.make_async_copy(gains_h, gains, loc.at[4])
     load_gains.start()
     load_wu.start()
@@ -95,48 +91,42 @@
                 greet(place(s, y, z + dz, (core + dc) % 2))
     for dy in range(1, n_y):
         greet(place(s, (y + dy) % n_y, z, core))
-    for step in (-2, 0, 1, 2, 3):
-        @pl.when(jnp.logical_not(first))
-        def _():
-            greet(place(s - 1, y, z + e * step, core))
-
-        @pl.when(jnp.logical_not(last))
-        def _():
-            greet(place(s + 1, y, z + e * step, core))
-
-    within = 2 * RING - 1 + n_y - 1
-    edge = jnp.logical_or(first, last)
-
-    @pl.when(edge)
-    def _():
-        pl.semaphore_wait(barrier, within + 5 * (sections > 1))
-
-    @pl.when(jnp.logical_not(edge))
-    def _():
-        pl.semaphore_wait(barrier, within + 10)
-
-    peers = ((3, 3), (2, -2), (1, 1))
-
-    def gather(buf, m, ssem, rsem):
-        for slot, step in peers:
-            send(
-                buf.at[m, pl.ds(0, rows)], buf.at[m, pl.ds(slot * rows, rows)],
-                ssem.at[m], rsem.at[m], place(s, y, z + e * step, core),
-            )
-
-    def scatter(src, dst, m, ssem, rsem, section):
+    for ds in range(1, sections):
+        for step in (-2, 0, 1, 2, 3):
+            greet(place((s + ds) % sections, y, z + e * step, core))
+    pl.semaphore_wait(barrier, 2 * RING - 1 + n_y - 1 + 5 * (sections - 1))
+
+    def gather(src, dst, ssem, rsem, section, slots=((3, 3), (2, -2), (1, 1), (0, 0))):
+        for slot, step in slots:
+            send(src, dst.at[pl.ds(slot * rows, rows)], ssem, rsem, place(section, y, z + e * step, core))
+
+    def scatter(src, dst, ssem, rsem, section):
         for slot in (3, 2, 1, 0):
-            send(
-                src.at[m, pl.ds(slot * rows, rows)], dst.at[m, slot],
-                ssem.at[m], rsem.at[m], place(section, y, z + e * slot, core),
-            )
+            send(src.at[pl.ds(slot * rows, rows)], dst.at[slot], ssem, rsem, place(section, y, z + e * slot, core))
+
+    def relay(part, total_ref, part_r, ssem, dst, rsem, section):
+        wait(part, part_r)
+        total = part[0].astype(F32)
+        for slot in range(1, 4):
+            total = total + part[slot].astype(F32)
+        total_ref[...] = total.astype(BF16)
+        gather(total_ref, dst, ssem, rsem, section)
+
+    def relay_f(duty, m, section):
+        at = duty * micro + m
+        relay(part_f.at[at], sum_f.at[at], rsf_r.at[at], agf_s.at[at], h_full.at[m], agf_r.at[m], section)
+
+    def relay_b(m, section):
+        relay(part_b.at[m], sum_b.at[m], rsb_r.at[m], agb_s.at[m], g_full.at[m], agb_r.at[m], section)
+
+    ring_y = sorted(range(1, n_y), key=lambda dy: -min(dy, n_y - dy))
 
     def to_y(buf, m, ssem, rsem):
-        for dy in range(1, n_y):
+        for dy in ring_y:
             send(buf.at[m, 0], buf.at[m, dy], ssem.at[m], rsem.at[m], place(s, (y + dy) % n_y, z, core))
 
     def cols_to_y(src, buf, m, ssem, rsem):
-        for dy in range(1, n_y):
+        for dy in ring_y:
             y_at = (y + dy) % n_y
             send(
                 src.at[m, :, pl.ds(pl.multiple_of(y_at * span, span), span)], buf.at[m, dy],
@@ -145,19 +135,8 @@
 
     own_cols = pl.ds(pl.multiple_of(y * span, span), span)
 
-    def rows_f(m):
-        @pl.when(jnp.logical_not(first))
-        def _():
-            wait(part_f.at[m], rsf_r.at[m])
-            total = part_f[m, 0].astype(F32)
-            for slot in range(1, 4):
-                total = total + part_f[m, slot].astype(F32)
-            h_full[m, pl.ds(0, rows)] = total.astype(BF16)
-
-        gather(h_full, m, agf_s, agf_r)
-
     def step_f(m):
-        wait(h_full.at[m, pl.ds(rows, 3 * rows)], agf_r.at[m])
+        wait(h_full.at[m], agf_r.at[m])
         hidden = h_full[m].astype(F32)
         normed, scale = stats(hidden)
         norm = (normed * gain_row).astype(BF16)
@@ -172,7 +151,13 @@
             mixed = dot(act, wd[...], (1, 0))
             send_f[m, pl.ds(0, rows)] = (mixed[:rows] + hidden[:rows]).astype(BF16)
             send_f[m, pl.ds(rows, 3 * rows)] = mixed[rows:].astype(BF16)
-            scatter(send_f, part_f, m, rsf_s, rsf_r, s + 1)
+            at = s // 2 * micro + m
+
+            @pl.when(m > 0)
+            def _():
+                wait(h_full.at[m - 1], rsf_s.at[m - 1])
+
+            scatter(send_f.at[m], part_f.at[at], rsf_s.at[m], rsf_r.at[at], (s + 3) % 4 - s // 2)
 
         slope_s[m] = 0.5 * (1.0 + tangent) + 0.5 * preact * (1.0 - tangent * tangent) * ROOT * (
             1.0 + 3.0 * COEF * preact * preact
@@ -184,20 +169,23 @@
         cols_to_y(norm_s, nc_all, m, nc_ss, nc_r)
         to_y(act_all, m, act_ss, act_r)
 
-    @pl.when(first)
-    def _():
-        pltpu.make_async_copy(inp, h_full.at[:, pl.ds(0, rows)], loc.at[2]).wait()
-
-    @pl.when(jnp.logical_not(last))
-    def _():
-        rows_f(0)
-
-    @pl.when(last)
-    def _():
-        pltpu.make_async_copy(og, g_full.at[:, pl.ds(0, rows)], loc.at[3]).wait()
-        for m in range(micro):
-            gather(g_full, m, agb_s, agb_r)
-
+    load_in.wait()
+    far = ((3, 3), (2, -2), (1, 1))
+
+    def spread(which, dst, rsem, section):
+        gather(own.at[which], dst.at[s], own_s.at[which], rsem.at[s], section, far)
+
+        @pl.when(s == section)
+        def _():
+            pltpu.make_async_copy(own.at[which], dst.at[s, pl.ds(0, rows)], rsem.at[s]).start()
+
+        @pl.when(s != section)
+        def _():
+            gather(own.at[which], dst.at[s], own_s.at[which], rsem.at[s], section, ((0, 0),))
+
+    spread(0, h_full, agf_r, 0)
+    load_og.wait()
+    spread(1, g_full, agb_r, sections - 1)
     load_gains.wait()
     load_wu.wait()
     load_wd.wait()
@@ -205,18 +193,8 @@
 
     gain_acc[...] = jnp.zeros_like(gain_acc)
 
-    def rows_b(m):
-        @pl.when(jnp.logical_not(last))
-        def _():
-            wait(part_b.at[m], rsb_r.at[m])
-            total = part_b[m, 0].astype(F32)
-            for slot in range(1, 4):
-                total = total + part_b[m, slot].astype(F32)
-            g_full[m, pl.ds(0, rows)] = total.astype(BF16)
-            gather(g_full, m, agb_s, agb_r)
-
     def step_b(m):
-        wait(g_full.at[m, pl.ds(rows, 3 * rows)], agb_r.at[m])
+        wait(g_full.at[m], agb_r.at[m])
         grad = g_full[m]
         down_grad = dot(grad, wd_t[...], (1, 0))
         pg = (down_grad * slope_s[m]).astype(BF16)
@@ -237,7 +215,7 @@
             )
             send_b[m, pl.ds(0, rows)] = (back[:rows] + grad[:rows].astype(F32)).astype(BF16)
             send_b[m, pl.ds(rows, 3 * rows)] = back[rows:].astype(BF16)
-            scatter(send_b, part_b, m, rsb_s, rsb_r, s - 1)
+            scatter(send_b.at[m], part_b.at[m], rsb_s.at[m], rsb_r.at[m], (s + 1) % 4 + s // 3)
 
         terms = norm_grad * normed
         total = terms[0:8]
@@ -261,34 +239,49 @@
         transpose(wd, wd_t)
         transpose(wu, wu_t)
 
+    def helping(start, stop, body):
+        def run(m, carry):
+            body(m)
+            return carry
+
+        lax.fori_loop(start, stop, run, 0)
+
+    @pl.when(last)
+    def _():
+        helping(0, micro, lambda m: relay_f(0, m, 1))
+
     turn = s // (sections - 1)
 
     def step(i, carry):
         back = turn * (i % 2) + (1 - turn) * (i // micro)
         m = turn * (i // 2) + (1 - turn) * (i % micro)
-        ahead = m + 1 - turn
 
         @pl.when(back == 0)
         def _():
-            @pl.when(ahead < micro)
-            def _():
-                rows_f(ahead)
-
             step_f(m)
 
         @pl.when(back == 1)
         def _():
             @pl.when(jnp.logical_and(first, m == 0))
             def _():
+                helping(0, micro, lambda m: relay_f(0, m, 2))
+                helping(0, micro, lambda m: relay_f(1, m, 3))
                 transpose(wd, wd_t)
                 transpose(wu, wu_t)
 
-            rows_b(m)
+            @pl.when(jnp.logical_and(s == 1, m == 0))
+            def _():
+                helping(0, micro, lambda m: relay_b(m, 2))
+
             step_b(m)
 
         return carry
 
     lax.fori_loop(0, 2 * micro, step, 0)
+
+    @pl.when(s >= 2)
+    def _():
+        helping(0, micro, lambda m: relay_b(m, s - 2))
 
     total = jnp.sum(gain_acc[...], axis=0, keepdims=True)
     lines = width // 128
@@ -377,16 +370,24 @@
     up_o[0] = finish(up_acc, up_buf, up2_r)
 
     def drain(m, carry):
-        wait(h_full.at[m, pl.ds(rows, 3 * rows)], agf_s.at[m])
-        wait(g_full.at[m, pl.ds(rows, 3 * rows)], agb_s.at[m])
+        @pl.when(jnp.logical_or(first, last))
+        def _():
+            wait(h_full.at[m], agf_s.at[m])
+
+        @pl.when(first)
+        def _():
+            wait(h_full.at[m], agf_s.at[micro + m])
 
         @pl.when(jnp.logical_not(last))
         def _():
-            wait(part_f.at[m], rsf_s.at[m])
+            @pl.when(m == micro - 1)
+            def _():
+                wait(h_full.at[m], rsf_s.at[m])
 
         @pl.when(jnp.logical_not(first))
         def _():
-            wait(part_b.at[m], rsb_s.at[m])
+            wait(g_full.at[m], agb_s.at[m])
+            wait(g_full.at[m], rsb_s.at[m])
 
         if n_y > 1:
             wait(act_all.at[m, pl.ds(1, n_y - 1)], act_ss.at[m])
@@ -396,6 +397,13 @@
         return carry
 
     lax.fori_loop(0, micro, drain, 0)
+    for which, section in ((0, 0), (1, sections - 1)):
+        wait(h_full.at[0, pl.ds(0, 3 * rows)], own_s.at[which])
+
+        @pl.when(s != section)
+        def _():
+            wait(h_full.at[0, pl.ds(0, rows)], own_s.at[which])
+
     if n_y > 1:
         wait(g1.at[pl.ds(1, n_y - 1)], g1_ss.at[0])
     wait(g2.at[pl.ds(1, 2 * RING - 1)], g2_ss.at[0])
@@ -403,6 +411,12 @@
     wait(up_buf.at[pl.ds(0, 2)], up_ss.at[0])
     wait(dn_buf.at[4], dn2_ss.at[0])
     wait(up_buf.at[4], up2_ss.at[0])
+
+
+def settle(up, down, gain, up_o, down_o, gain_o):
+    up_o[...] = up[...]
+    down_o[...] = down[...]
+    gain_o[...] = gain[...]
 
 
 def solution(mesh):
@@ -432,11 +446,14 @@
             scratch_shapes=[
                 pltpu.VMEM((width, hid), BF16),
                 pltpu.VMEM((hid, width), BF16),
+                pltpu.VMEM((2, rows, width), BF16),
                 pltpu.VMEM((micro, full, width), BF16),
-                pltpu.VMEM((micro, 4, rows, width), BF16),
+                pltpu.VMEM((2 * micro, 4, rows, width), BF16),
+                pltpu.VMEM((2 * micro, rows, width), BF16),
                 pltpu.VMEM((micro, full, width), BF16),
                 pltpu.VMEM((micro, full, width), BF16),
                 pltpu.VMEM((micro, 4, rows, width), BF16),
+                pltpu.VMEM((micro, rows, width), BF16),
                 pltpu.VMEM((micro, full, width), BF16),
                 pltpu.VMEM((1, width), F32),
                 pltpu.VMEM((micro, full, width), F32),
@@ -457,11 +474,18 @@
                 pltpu.VMEM((n_y, width // 128, 128), F32),
                 pltpu.VMEM((2 * RING, width // 128, 128), F32),
                 dma((5,)),
-            ] + [many] * 16 + [one] * 12,
+                dma((2,)), dma((2 * micro,)), many, many, dma((2 * micro,)),
+            ] + [many] * 12 + [one] * 12,
             compiler_params=pltpu.CompilerParams(
                 collective_id=0, has_side_effects=True, vmem_limit_bytes=63 * 1024 * 1024
             ),
         )(inputs, gains, w_up, w_down, out_grad)
+        up, down, gain = pl.pallas_call(
+            settle,
+            out_shape=tuple(jax.ShapeDtypeStruct(part.shape, F32) for part in (up, down, gain)),
+            in_specs=[vmem] * 3,
+            out_specs=(vmem,) * 3,
+        )(up, down, gain)
         return up, jnp.swapaxes(down, 1, 2), gain
 
     return jax.shard_map(

time: 144 us -> 134 us (0.931)
  Pallas kernels: 139 us -> 133 us
  local copies, waits for them, and re-layouts: 4.45 us -> 0 us
    pallas_call x1, Pallas kernels: 139 us -> 131 us  [per_device(): pl.pallas_call(functools.partial(kernel, sections=sections, n_y=n_y), out...]
    unnamed x3 -> x0, local copies, waits for them, and re-layouts: 4.45 us -> none
    pallas_call x0 -> x1, Pallas kernels: none -> 1.84 us  [per_device(): pl.pallas_call(settle, out_shape=tuple((jax.ShapeDtypeStruct(part.shape,...]
where the time goes in v3:
time: 134 us
  Pallas kernels  133 us (99%)
    pallas_call x1, Pallas kernels, per_device(): pl.pallas_call(functools.partial(kernel, sections=sections, n_y=n_y), out...  131 us

profile of v3, /device:TPU:1, one launch (start us, length us, event | category | flops | bytes accessed | tf_op | source)
XLA Modules:
  0.0 133.6 jit_solution(6001172091064694777)
XLA Ops:
  0.6 131.1 %shard_map.76 = (f32[1,64,1024]{2,1,0:T(8,128)}, f32[1,64,1024]{2,1,0:T(8,128)}, f32[1,16]{1,0:T(1,128)}) custom-call(bf16[4,16,1024]{2,1,0:T(8,128)(2,1)} %inp.1, f32[1,1024]{1,0:T(1,128)} %gains_h.1, bf16[1,1024,1024]{2,1,0:T(8,128)(2,1)} %wu_h.1, bf16[1,1024,1024]{2,1,0:T(8,128)(2,1)} %wd_h.1, bf16[4,16,1024]{2,1,0:T(8,128)(2,1)} %og.1), custom_call_target="tpu_custom_call" | custom-call | tf_op jit(solution)/shard_map/pallas_call | solution.py:437
  131.8 1.8 %shard_map.77 = (f32[1,64,1024]{2,1,0:T(8,128)}, f32[1,64,1024]{2,1,0:T(8,128)}, f32[1,16]{1,0:T(1,128)}) custom-call(f32[1,64,1024]{2,1,0:T(8,128)} %get-tuple-element.9.up, f32[1,64,1024]{2,1,0:T(8,128)} %get-tuple-element.10.down, f32[1,16]{1,0:T(1,128)} %get-tuple-element.11.gain), custom_call_target="tpu_custom_call" | custom-call | tf_op jit(solution)/shard_map/pallas_call | solution.py:483

commit v4 on v3

--- a/solution.py
+++ b/solution.py
@@ -125,6 +125,18 @@
         for dy in ring_y:
             send(buf.at[m, 0], buf.at[m, dy], ssem.at[m], rsem.at[m], place(s, (y + dy) % n_y, z, core))
 
+    hid = pg_all.shape[3]
+    whole = pl.ds(0, hid)
+    halves = (pl.ds(0, hid // 2), pl.ds(hid // 2, hid // 2))
+
+    def pg_to_y(m):
+        for half, cols in enumerate(halves):
+            for dy in ring_y:
+                send(
+                    pg_all.at[m, 0, :, cols], pg_all.at[m, dy, :, cols],
+                    pg_ss.at[m], pg_r.at[2 * m + half], place(s, (y + dy) % n_y, z, core),
+                )
+
     def cols_to_y(src, buf, m, ssem, rsem):
         for dy in ring_y:
             y_at = (y + dy) % n_y
@@ -157,7 +169,7 @@
             def _():
                 wait(h_full.at[m - 1], rsf_s.at[m - 1])
 
-            scatter(send_f.at[m], part_f.at[at], rsf_s.at[m], rsf_r.at[at], (s + 3) % 4 - s // 2)
+            scatter(send_f.at[m], part_f.at[at], rsf_s.at[m], rsf_r.at[at], (s + 3) % 4)
 
         slope_s[m] = 0.5 * (1.0 + tangent) + 0.5 * preact * (1.0 - tangent * tangent) * ROOT * (
             1.0 + 3.0 * COEF * preact * preact
@@ -196,12 +208,12 @@
     def step_b(m):
         wait(g_full.at[m], agb_r.at[m])
         grad = g_full[m]
+        gc_all[m, 0] = g_full[m, :, own_cols]
+        cols_to_y(g_full, gc_all, m, gc_ss, gc_r)
         down_grad = dot(grad, wd_t[...], (1, 0))
         pg = (down_grad * slope_s[m]).astype(BF16)
         pg_all[m, 0] = pg
-        to_y(pg_all, m, pg_ss, pg_r)
-        gc_all[m, 0] = g_full[m, :, own_cols]
-        cols_to_y(g_full, gc_all, m, gc_ss, gc_r)
+        pg_to_y(m)
         norm_grad = dot(pg, wu_t[...], (1, 0))
         normed = normed_s[m]
 
@@ -265,12 +277,12 @@
             @pl.when(jnp.logical_and(first, m == 0))
             def _():
                 helping(0, micro, lambda m: relay_f(0, m, 2))
-                helping(0, micro, lambda m: relay_f(1, m, 3))
                 transpose(wd, wd_t)
                 transpose(wu, wu_t)
 
             @pl.when(jnp.logical_and(s == 1, m == 0))
             def _():
+                helping(0, micro, lambda m: relay_f(1, m, 3))
                 helping(0, micro, lambda m: relay_b(m, 2))
 
             step_b(m)
@@ -301,12 +313,18 @@
         dn_acc[...] += dot(cols, act_all[m].reshape(n_y * full, -1), (0, 0))
         return carry
 
+    def up_half(m, half):
+        cols = halves[half]
+        if n_y > 1:
+            wait(pg_all.at[m, pl.ds(1, n_y - 1), :, cols], pg_r.at[2 * m + half])
+        left = nc_all[m].reshape(n_y * full, span)
+        up_acc[:, cols] += dot(left, pg_all[m, :, :, cols].reshape(n_y * full, -1), (0, 0))
+
     def up_part(m, carry):
         if n_y > 1:
             wait(nc_all.at[m, pl.ds(1, n_y - 1)], nc_r.at[m])
-            wait(pg_all.at[m, pl.ds(1, n_y - 1)], pg_r.at[m])
-        cols = nc_all[m].reshape(n_y * full, span)
-        up_acc[...] += dot(cols, pg_all[m].reshape(n_y * full, -1), (0, 0))
+        for half in range(2):
+            up_half(m, half)
         return carry
 
     other = 1 - core
@@ -314,24 +332,26 @@
     def block(z_lo_at, core_at):
         return pl.ds(pl.multiple_of((z_lo_at * 2 + core_at) * share, share), share)
 
-    def to_core(acc, buf, ssem, rsem):
+    def to_core(acc, buf, ssem, rsem, cols):
         for z_lo_at in range(2):
-            buf[z_lo_at] = acc[block(z_lo_at, other)].astype(BF16)
-        send(buf.at[pl.ds(0, 2)], buf.at[pl.ds(2, 2)], ssem.at[0], rsem.at[0], place(s, y, z, other))
-
-    def to_pair(acc, buf, rsem, ssem2, rsem2):
-        wait(buf.at[pl.ds(2, 2)], rsem.at[0])
+            buf[z_lo_at, :, cols] = acc[block(z_lo_at, other), cols].astype(BF16)
+        send(buf.at[pl.ds(0, 2), :, cols], buf.at[pl.ds(2, 2), :, cols], ssem, rsem, place(s, y, z, other))
+
+    def to_pair(acc, buf, rsem, ssem2, rsem2, cols):
+        wait(buf.at[pl.ds(2, 2), :, cols], rsem)
         away = 1 - z_lo
-        buf[4] = (acc[block(away, core)] + buf[2 + away].astype(F32)).astype(BF16)
-        send(buf.at[4], buf.at[5], ssem2.at[0], rsem2.at[0], place(s, y, 2 * t + away, core))
-
-    def finish(acc, buf, rsem2):
-        wait(buf.at[5], rsem2.at[0])
-        return acc[block(z_lo, core)] + buf[2 + z_lo].astype(F32) + buf[5].astype(F32)
+        buf[4, :, cols] = (acc[block(away, core), cols] + buf[2 + away, :, cols].astype(F32)).astype(BF16)
+        send(buf.at[4, :, cols], buf.at[5, :, cols], ssem2, rsem2, place(s, y, 2 * t + away, core))
+
+    def finish(acc, buf, rsem2, cols):
+        wait(buf.at[5, :, cols], rsem2)
+        return acc[block(z_lo, core), cols] + buf[2 + z_lo, :, cols].astype(F32) + buf[5, :, cols].astype(F32)
+
+    lax.fori_loop(0, micro, down_part, 0)
+    to_core(dn_acc, dn_buf, dn_ss.at[0], dn_r.at[0], whole)
 
     lax.fori_loop(0, micro - 1, up_part, 0)
-    lax.fori_loop(0, micro, down_part, 0)
-    to_core(dn_acc, dn_buf, dn_ss, dn_r)
+    to_pair(dn_acc, dn_buf, dn_r.at[0], dn2_ss.at[0], dn2_r.at[0], whole)
 
     if n_y > 1:
         wait(g1.at[pl.ds(1, n_y - 1)], g1_r.at[0])
@@ -347,11 +367,13 @@
                     place(s, y, z + dz, (core + dc) % 2),
                 )
 
-    to_pair(dn_acc, dn_buf, dn_r, dn2_ss, dn2_r)
-    up_part(micro - 1, 0)
-    to_core(up_acc, up_buf, up_ss, up_r)
-    to_pair(up_acc, up_buf, up_r, up2_ss, up2_r)
-    dn_o[0] = finish(dn_acc, dn_buf, dn2_r)
+    if n_y > 1:
+        wait(nc_all.at[micro - 1, pl.ds(1, n_y - 1)], nc_r.at[micro - 1])
+    for half, cols in enumerate(halves):
+        up_half(micro - 1, half)
+        to_core(up_acc, up_buf, up_ss.at[half], up_r.at[half], cols)
+        to_pair(up_acc, up_buf, up_r.at[half], up2_ss.at[half], up2_r.at[half], cols)
+    dn_o[0] = finish(dn_acc, dn_buf, dn2_r.at[0], whole)
 
     wait(g2.at[pl.ds(1, 2 * RING - 1)], g2_r.at[0])
     total = g2[0]
@@ -367,14 +389,15 @@
         piece = piece + jnp.where(index % fold == at, line[:, at * per:(at + 1) * per], 0.0)
     gain_o[...] = piece
 
-    up_o[0] = finish(up_acc, up_buf, up2_r)
+    for half, cols in enumerate(halves):
+        up_o[0, :, cols] = finish(up_acc, up_buf, up2_r.at[half], cols)
 
     def drain(m, carry):
         @pl.when(jnp.logical_or(first, last))
         def _():
             wait(h_full.at[m], agf_s.at[m])
 
-        @pl.when(first)
+        @pl.when(s == 1)
         def _():
             wait(h_full.at[m], agf_s.at[micro + m])
 
@@ -408,9 +431,10 @@
         wait(g1.at[pl.ds(1, n_y - 1)], g1_ss.at[0])
     wait(g2.at[pl.ds(1, 2 * RING - 1)], g2_ss.at[0])
     wait(dn_buf.at[pl.ds(0, 2)], dn_ss.at[0])
-    wait(up_buf.at[pl.ds(0, 2)], up_ss.at[0])
+    for half, cols in enumerate(halves):
+        wait(up_buf.at[pl.ds(0, 2), :, cols], up_ss.at[half])
+        wait(up_buf.at[4, :, cols], up2_ss.at[half])
     wait(dn_buf.at[4], dn2_ss.at[0])
-    wait(up_buf.at[4], up2_ss.at[0])
 
 
 def settle(up, down, gain, up_o, down_o, gain_o):
@@ -475,7 +499,7 @@
                 pltpu.VMEM((2 * RING, width // 128, 128), F32),
                 dma((5,)),
                 dma((2,)), dma((2 * micro,)), many, many, dma((2 * micro,)),
-            ] + [many] * 12 + [one] * 12,
+            ] + [many] * 9 + [dma((2 * micro,))] + [many] * 2 + [dma((2,))] * 12,
             compiler_params=pltpu.CompilerParams(
                 collective_id=0, has_side_effects=True, vmem_limit_bytes=63 * 1024 * 1024
             ),

time: 134 us -> 131 us (0.978)
  Pallas kernels: 133 us -> 131 us
    pallas_call x1, Pallas kernels: 131 us -> 129 us  [per_device(): pl.pallas_call(functools.partial(kernel, sections=sections, n_y=n_y), out...]
where the time goes in v4:
time: 131 us
  Pallas kernels  131 us (100%)
    pallas_call x1, Pallas kernels, per_device(): pl.pallas_call(functools.partial(kernel, sections=sections, n_y=n_y), out...  129 us

profile of v4, /device:TPU:1, one launch (start us, length us, event | category | flops | bytes accessed | tf_op | source)
XLA Modules:
  0.0 131.3 jit_solution(16731422291087896884)
XLA Ops:
  0.6 128.8 %shard_map.76 = (f32[1,64,1024]{2,1,0:T(8,128)}, f32[1,64,1024]{2,1,0:T(8,128)}, f32[1,16]{1,0:T(1,128)}) custom-call(bf16[4,16,1024]{2,1,0:T(8,128)(2,1)} %inp.1, f32[1,1024]{1,0:T(1,128)} %gains_h.1, bf16[1,1024,1024]{2,1,0:T(8,128)(2,1)} %wu_h.1, bf16[1,1024,1024]{2,1,0:T(8,128)(2,1)} %wd_h.1, bf16[4,16,1024]{2,1,0:T(8,128)(2,1)} %og.1), custom_call_target="tpu_custom_call" | custom-call | tf_op jit(solution)/shard_map/pallas_call | solution.py:461
  129.5 1.8 %shard_map.77 = (f32[1,64,1024]{2,1,0:T(8,128)}, f32[1,64,1024]{2,1,0:T(8,128)}, f32[1,16]{1,0:T(1,128)}) custom-call(f32[1,64,1024]{2,1,0:T(8,128)} %get-tuple-element.9.up, f32[1,64,1024]{2,1,0:T(8,128)} %get-tuple-element.10.down, f32[1,16]{1,0:T(1,128)} %get-tuple-element.11.gain), custom_call_target="tpu_custom_call" | custom-call | tf_op jit(solution)/shard_map/pallas_call | solution.py:507

commit v5 on v4

--- a/solution.py
+++ b/solution.py
@@ -504,11 +504,14 @@
                 collective_id=0, has_side_effects=True, vmem_limit_bytes=63 * 1024 * 1024
             ),
         )(inputs, gains, w_up, w_down, out_grad)
+        piece = pl.BlockSpec((1, share // 2, hid), lambda at: (0, at, 0))
+        line = pl.BlockSpec((1, per), lambda at: (0, 0))
         up, down, gain = pl.pallas_call(
             settle,
             out_shape=tuple(jax.ShapeDtypeStruct(part.shape, F32) for part in (up, down, gain)),
-            in_specs=[vmem] * 3,
-            out_specs=(vmem,) * 3,
+            grid=(2,),
+            in_specs=[piece, piece, line],
+            out_specs=(piece, piece, line),
         )(up, down, gain)
         return up, jnp.swapaxes(down, 1, 2), gain
 

time: 131 us -> 131 us (level)
  no operation moved by 1% of the time
where the time goes in v5:
time: 131 us
  Pallas kernels  131 us (100%)
    pallas_call x1, Pallas kernels, per_device(): pl.pallas_call(functools.partial(kernel, sections=sections, n_y=n_y), out...  129 us

profile of v5, /device:TPU:1, one launch (start us, length us, event | category | flops | bytes accessed | tf_op | source)
XLA Modules:
  0.0 131.3 jit_solution(3782147686128319411)
XLA Ops:
  0.6 128.8 %shard_map.76 = (f32[1,64,1024]{2,1,0:T(8,128)}, f32[1,64,1024]{2,1,0:T(8,128)}, f32[1,16]{1,0:T(1,128)}) custom-call(bf16[4,16,1024]{2,1,0:T(8,128)(2,1)} %inp.1, f32[1,1024]{1,0:T(1,128)} %gains_h.1, bf16[1,1024,1024]{2,1,0:T(8,128)(2,1)} %wu_h.1, bf16[1,1024,1024]{2,1,0:T(8,128)(2,1)} %wd_h.1, bf16[4,16,1024]{2,1,0:T(8,128)(2,1)} %og.1), custom_call_target="tpu_custom_call" | custom-call | tf_op jit(solution)/shard_map/pallas_call | solution.py:461
  129.5 1.8 %shard_map.77 = (f32[1,64,1024]{2,1,0:T(8,128)}, f32[1,64,1024]{2,1,0:T(8,128)}, f32[1,16]{1,0:T(1,128)}) custom-call(f32[1,64,1024]{2,1,0:T(8,128)} %get-tuple-element.9.up, f32[1,64,1024]{2,1,0:T(8,128)} %get-tuple-element.10.down, f32[1,16]{1,0:T(1,128)} %get-tuple-element.11.gain), custom_call_target="tpu_custom_call" | custom-call | tf_op jit(solution)/shard_map/pallas_call | solution.py:509
